TPU v7x, 256 devices: a whole 4x4x8 slice. The times are simulated.
256 devices in a mesh: freq: 16 (over y_hi, x, core), recv: 16 (over y_lo, z).
Axes of the slice: x: 4, y: 4 (y_hi: 2, y_lo: 2; y = y_hi * 2 + y_lo), z: 8, core: 2. Of those that a mesh axis runs over, the one named last changes fastest.
Arguments:
- response: bfloat16 [2, 256, 512, 4096], P(None, 'freq', 'recv'), may hold values from -0.0625 to 0.0625
- focusing: float32 [2, 256, 16, 4096], P(None, 'freq', None, 'recv'), may hold values from -6 to 6
- window_onset: int32 [16, 512], P(None, ('recv', 'freq')), may hold values from 0 to 511
- window_end: int32 [16, 512], P(None, ('recv', 'freq')), may hold values from 128 to 1023, as said below
Outputs:
- windowed: float32 [16, 512, 1024], P(None, ('recv', 'freq'))
Inputs may be any that keep to these rules, and one draw needn't show every extreme that they name: window_end - window_onset lies between 128 and 512 for every trace.
All inputs are finite; a program needn't handle non-finite values.
Results may differ from a plain program's by a relative error of at most 0.0029.
Values may be sent and summed in bfloat16 or wider, within the bound.
No kernel may reach another device: no remote copies, remote signals or barrier semaphores. Data moves between devices by JAX's collectives and lax.ppermute only.
A program may use at most 64 MiB of HBM per device.

v0:
```python
import math
import jax
import jax.numpy as jnp
from jax import lax
from jax.sharding import PartitionSpec as P

NF = 256
NT = 1024


def make_table(count):
    freqs = jnp.arange(count, dtype=jnp.int32)
    samples = jnp.arange(NT, dtype=jnp.int32)
    phase = (freqs[:, None] * samples[None, :] % NT).astype(jnp.float32) * (2.0 * math.pi / NT)
    scale = 1.0 / math.sqrt(NF)
    return jnp.concatenate([jnp.cos(phase) * scale, -jnp.sin(phase) * scale], 0)


def transform(stacked, table):
    return lax.dot_general(
        stacked,
        table,
        (((0,), (0,)), ((), ())),
        precision=lax.Precision.HIGHEST,
        preferred_element_type=jnp.float32,
    )


def per_device(response, focusing, window_onset, window_end):
    focal = focusing.shape[2]
    focus_half = focusing.astype(jnp.bfloat16)
    gathered = lax.all_gather(focus_half, "recv", axis=3, tiled=True)
    real_part = jnp.einsum(
        "krs,kqs->krq", response[0], gathered[0], preferred_element_type=jnp.float32
    )
    real_part = real_part - jnp.einsum(
        "krs,kqs->krq", response[1], gathered[1], preferred_element_type=jnp.float32
    )
    imag_part = jnp.einsum(
        "krs,kqs->krq", response[0], gathered[1], preferred_element_type=jnp.float32
    )
    imag_part = imag_part + jnp.einsum(
        "krs,kqs->krq", response[1], gathered[0], preferred_element_type=jnp.float32
    )
    spectra = jnp.stack([real_part, imag_part])
    owned = window_onset.shape[1]
    moved = lax.all_to_all(spectra, "freq", split_axis=2, concat_axis=1, tiled=True)
    flat = moved.reshape(2 * NF, owned * focal)
    traces = transform(flat, make_table(NF))
    traces = jnp.transpose(traces.reshape(owned, focal, NT), (1, 0, 2))
    samples = jnp.arange(NT, dtype=jnp.int32)
    keep = (samples[None, None, :] >= window_onset[:, :, None]) & (
        samples[None, None, :] < window_end[:, :, None]
    )
    return jnp.where(keep, traces, jnp.float32(0.0))


def solution(mesh):
    in_specs = (
        P(None, "freq", "recv", None),
        P(None, "freq", None, "recv"),
        P(None, ("recv", "freq")),
        P(None, ("recv", "freq")),
    )
    out_specs = P(None, ("recv", "freq"), None)
    return jax.shard_map(
        per_device, mesh=mesh, in_specs=in_specs, out_specs=out_specs, check_vma=False
    )
```

profile of v0, /device:TPU:1, one launch (start us, length us, event | category | flops | bytes accessed | tf_op | source)
XLA Modules:
  0.0 139.6 jit_solution(12699561626764175694)
XLA Ops:
  6.5 0.0 all-gather.2.cloned.1.call-start
  6.5 1.8 %convert_element_type.8 = bf16[2,16,16,256]{3,2,1,0:T(8,128)(2,1)} convert(f32[2,16,16,256]{3,2,1,0:T(8,128)} %param.5) | non-fusion elementwise | flops 131072 | bytes 786432 | tf_op jit(solution)/shard_map/convert_element_type | solution.py:31
  8.3 0.0 all-gather.2.cloned.1.call-update
  8.3 84.3 %all-gather.2.cloned.1.call-done = bf16[2,16,16,4096]{3,2,1,0:T(8,128)(2,1)} async-done(((bf16[2,16,16,256]{3,2,1,0:T(8,128)(2,1)}), bf16[2,16,16,4096]{3,2,1,0:T(8,128)(2,1)}) %all-gather.2.cloned.1.call-update) | async-done | bytes 4194320 | tf_op jit(solution)/shard_map/all_gather | solution.py:32
  92.7 4.2 %fusion.2 = f32[16,32,16]{1,2,0:T(8,128)S(1)} fusion(bf16[2,16,32,4096]{3,2,1,0:T(8,128)(2,1)} %param.4, bf16[2,16,16,4096]{3,2,1,0:T(8,128)(2,1)} %all-gather.2.cloned.1.call-done), kind=kOutput, calls=%fused_computation.2 | convolution fusion | flops 67108864 | bytes 6324224 | tf_op jit(solution)/shard_map/krs,kqs->krq/dot_general | solution.py:36
  96.9 1.0 copy-done.2
  97.9 2.9 %fusion = f32[16,32,16]{1,2,0:T(8,128)S(1)} fusion(bf16[2,16,32,4096]{3,2,1,0:T(8,128)(2,1)S(1)} %copy-done.2, bf16[2,16,16,4096]{3,2,1,0:T(8,128)(2,1)} %all-gather.2.cloned.1.call-done), kind=kOutput, calls=%fused_computation | convolution fusion | flops 67108864 | bytes 6324224 | tf_op jit(solution)/shard_map/krs,kqs->krq/dot_general | solution.py:42
  100.8 1.2 fusion.20
  102.1 1.2 fusion.26
  103.3 0.0 copy-start
  103.3 0.0 copy-start.1
  103.3 0.5 copy.9
  103.8 0.9 reshape.10
  104.7 16.5 %all-to-all-start = ((f32[16,1,1024]{2,1,0:T(1,128)}), f32[16,1,1024]{2,1,0:T(1,128)S(1)}, u32[]{:S(2)}, u32[]{:S(2)}) async-start(f32[16,1,1024]{2,1,0:T(1,128)} %reshape.10), calls=%async_computation | async-start | bytes 131072 | tf_op jit(solution)/shard_map/all_to_all | solution.py:47
  121.1 4.1 %negate_multiply_fusion = (f32[256,1024]{1,0:T(8,128)S(1)}, f32[256,1024]{1,0:T(8,128)S(1)}) fusion(), kind=kLoop, calls=%fused_computation.30 | loop fusion | flops 4456448 | bytes 2097152 | tf_op jit(solution)/shard_map/mul | solution.py:16
  125.3 3.2 %all-to-all-done = f32[16,1,1024]{2,1,0:T(1,128)S(1)} async-done(((f32[16,1,1024]{2,1,0:T(1,128)}), f32[16,1,1024]{2,1,0:T(1,128)S(1)}, u32[]{:S(2)}, u32[]{:S(2)}) %all-to-all-start) | async-done | bytes 65568 | tf_op jit(solution)/shard_map/all_to_all | solution.py:47
  128.5 0.5 broadcast.20
  129.0 0.8 reduce
  129.8 0.2 reshape.11
  130.0 0.4 copy.11
  130.4 0.3 reshape.8
  130.7 0.0 copy-done
  130.7 1.3 fusion.16
  132.0 0.8 copy.12
  (5 shorter events, 0.0 us)
Async XLA Ops:
  6.5 86.1 %all-gather.2.cloned.1.call-start = ((), (), s32[]{:S(2)}) async-start(), calls=%async_computation.1 | async-start | bytes 4456448 | tf_op jit(solution)/shard_map/all_gather | solution.py:32
  92.7 5.2 %copy-start.2 = (bf16[2,16,32,4096]{3,2,1,0:T(8,128)(2,1)S(1)}, bf16[2,16,32,4096]{3,2,1,0:T(8,128)(2,1)}, u32[]{:S(2)}) copy-start(bf16[2,16,32,4096]{3,2,1,0:T(8,128)(2,1)} %param.4) | copy-start | bytes 25165828
  97.9 2.9 %copy-start.3 = (bf16[2,16,16,4096]{3,2,1,0:T(8,128)(2,1)S(1)}, bf16[2,16,16,4096]{3,2,1,0:T(8,128)(2,1)}, u32[]{:S(2)}) copy-start(bf16[2,16,16,4096]{3,2,1,0:T(8,128)(2,1)} %all-gather.2.cloned.1.call-done) | copy-start | bytes 12582916
  103.3 27.4 %copy-start = (s32[16,2]{0,1:T(2,128)S(1)}, s32[16,2]{0,1:T(2,128)}, u32[]{:S(2)}) copy-start(s32[16,2]{0,1:T(2,128)} %param.7) | copy-start | bytes 388
  103.3 27.4 %copy-start.1 = (s32[16,2]{0,1:T(2,128)S(1)}, s32[16,2]{0,1:T(2,128)}, u32[]{:S(2)}) copy-start(s32[16,2]{0,1:T(2,128)} %param.6) | copy-start | bytes 388
  104.7 23.8 %all-to-all-start = ((f32[16,1,1024]{2,1,0:T(1,128)}), f32[16,1,1024]{2,1,0:T(1,128)S(1)}, u32[]{:S(2)}, u32[]{:S(2)}) async-start(f32[16,1,1024]{2,1,0:T(1,128)} %reshape.10), calls=%async_computation | async-start | bytes 131072 | tf_op jit(solution)/shard_map/all_to_all | solution.py:47
Sparse Core Ops, SparseCore 0:
  9.1 83.5 all-gather.1
where the time goes:
time: 140 us
  waiting for transfers between devices  87.5 us (62%)
  starting transfers between devices  16.5 us (12%)
  between operations  13.5 us (10%)
  matrix products  10.9 us (8%)
  other arithmetic  6.75 us (5%)
  local copies, waits for them, and re-layouts  4.55 us (3%)
    all_gather x1, waiting for transfers between devices, per_device(): gathered = lax.all_gather(focus_half, 'recv', axis=3, tiled=True)  84.3 us
    all_to_all x1, starting transfers between devices, per_device(): lax.all_to_all(spectra, 'freq', split_axis=2, concat_axis=1, tiled=True)  16.5 us
    dot_general x1, matrix products, per_device(): jnp.einsum('krs,kqs->krq', response[1], gathered[1], preferred_element_ty...  4.2 us
    mul x1, other arithmetic, make_table(): return jnp.concatenate([jnp.cos(phase) * scale, -jnp.sin(phase) * scale], 0)  4.15 us
    all_to_all x1, waiting for transfers between devices, per_device(): lax.all_to_all(spectra, 'freq', split_axis=2, concat_axis=1, tiled=True)  3.18 us
    dot_general x1, matrix products, per_device(): jnp.einsum('krs,kqs->krq', response[1], gathered[0], preferred_element_ty...  2.94 us
  transfers between devices with their start and end apart: 2, of which 2 were waited for; matrix products, arithmetic and copies ran while one was open for 3% of the time, Pallas kernels for 0%

commit v1 on v0

--- a/solution.py
+++ b/solution.py
@@ -29,7 +29,9 @@
 def per_device(response, focusing, window_onset, window_end):
     focal = focusing.shape[2]
     focus_half = focusing.astype(jnp.bfloat16)
-    gathered = lax.all_gather(focus_half, "recv", axis=3, tiled=True)
+    gathered = jnp.concatenate(
+        lax.all_to_all(jnp.stack([focus_half] * lax.axis_size("recv")), "recv", 0, 0), axis=3
+    )
     real_part = jnp.einsum(
         "krs,kqs->krq", response[0], gathered[0], preferred_element_type=jnp.float32
     )

time: 140 us -> 150 us (1.071)
  blocking collectives: 0 us -> 102 us
  waiting for transfers between devices: 87.5 us -> 3.16 us
  between operations: 13.5 us -> 0.13 us
  local copies, waits for them, and re-layouts: 4.55 us -> 14.3 us
  starting transfers between devices: 16.5 us -> 9.57 us
  matrix products: 10.9 us -> 13.8 us
    all_to_all x0 -> x1, blocking collectives: none -> 102 us  [per_device(): lax.all_to_all(jnp.stack([focus_half] * lax.axis_size('recv')), 'recv', 0...]
    all_gather x1 -> x0, waiting for transfers between devices: 84.3 us -> none  [per_device(): gathered = lax.all_gather(focus_half, 'recv', axis=3, tiled=True)]
    all_to_all x1, starting transfers between devices: 16.5 us -> 9.57 us  [per_device(): lax.all_to_all(spectra, 'freq', split_axis=2, concat_axis=1, tiled=True)]
    slice x0 -> x3, local copies, waits for them, and re-layouts: none -> 5.6 us  [the longest x2 2.84 us: per_device(): gathered[1]]
    squeeze x0 -> x2, local copies, waits for them, and re-layouts: none -> 4.69 us  [the longest x1 2.35 us: per_device(): gathered[0]]
    dot_general x1, matrix products: 1.22 us -> 3.57 us  [per_device(): jnp.einsum('krs,kqs->krq', response[0], gathered[0], preferred_element_ty...]
  transfers between devices with their start and end apart: 2 -> 1, of which waited for: 2 -> 1; matrix products, arithmetic and copies ran while one was open for 3% -> 3% of each run, Pallas kernels for 0% -> 0%
where the time goes in v1:
time: 150 us; the launch traced here: 149 us
  blocking collectives  102 us (68%)
  local copies, waits for them, and re-layouts  14.3 us (10%)
  matrix products  13.8 us (9%)
  starting transfers between devices  9.57 us (6%)
  other arithmetic  6.05 us (4%)
  waiting for transfers between devices  3.16 us (2%)
    all_to_all x1, blocking collectives, per_device(): lax.all_to_all(jnp.stack([focus_half] * lax.axis_size('recv')), 'recv', 0...  102 us
    all_to_all x1, starting transfers between devices, per_device(): lax.all_to_all(spectra, 'freq', split_axis=2, concat_axis=1, tiled=True)  9.57 us
    dot_general x1, matrix products, per_device(): jnp.einsum('krs,kqs->krq', response[1], gathered[1], preferred_element_ty...  4.2 us
    mul x1, other arithmetic, make_table(): return jnp.concatenate([jnp.cos(phase) * scale, -jnp.sin(phase) * scale], 0)  4.15 us
    dot_general x1, matrix products, per_device(): jnp.einsum('krs,kqs->krq', response[0], gathered[0], preferred_element_ty...  3.57 us
    dot_general x1, matrix products, per_device(): jnp.einsum('krs,kqs->krq', response[1], gathered[0], preferred_element_ty...  3.56 us
    all_to_all x1, waiting for transfers between devices, per_device(): lax.all_to_all(spectra, 'freq', split_axis=2, concat_axis=1, tiled=True)  3.16 us
  transfers between devices with their start and end apart: 1, of which 1 were waited for; matrix products, arithmetic and copies ran while one was open for 3% of the time, Pallas kernels for 0%

profile of v1, /device:TPU:1, one launch (start us, length us, event | category | flops | bytes accessed | tf_op | source)
XLA Modules:
  0.0 149.3 jit_solution(13537201095776670759)
XLA Ops:
  0.0 1.1 convert_element_type.8
  1.1 0.5 stack.8
  1.5 102.3 %all_to_all.20 = bf16[16,2,16,16,256]{4,3,2,1,0:T(8,128)(2,1)S(1)} all-to-all(bf16[16,2,16,16,256]{4,3,2,1,0:T(8,128)(2,1)S(1)} %stack.8), channel_id=1, replica_groups=mesh['freq'=16,'recv'=16] {'recv'}, dimensions={0} | all-to-all | bytes 8388608 | tf_op jit(solution)/shard_map/all_to_all | solution.py:33
  103.9 1.6 %fusion.37 = (bf16[1,16,16,16,256]{4,2,1,0,3:T(8,128)(2,1)S(1)}, bf16[1,16,16,16,256]{4,2,1,0,3:T(8,128)(2,1)}) fusion(bf16[2,16,16,16,256]{4,2,1,0,3:T(8,128)(2,1)S(1)} %bitcast.55), kind=kLoop, calls=%fused_computation.38 | loop fusion | bytes 8388608 | tf_op jit(solution)/shard_map/slice | solution.py:39
  105.5 1.2 copy.10
  106.7 2.3 %squeeze.19 = bf16[16,16,4096]{2,1,0:T(8,128)(2,1)} reshape(bf16[1,16,16,16,256]{4,3,2,1,0:T(8,128)(2,1)S(1)} %copy.10) | data formatting | bytes 4194304 | tf_op jit(solution)/shard_map/squeeze | solution.py:39
  109.0 2.8 %copy.9 = bf16[1,16,16,16,256]{4,3,2,1,0:T(8,128)(2,1)S(1)} copy(bf16[1,16,16,16,256]{4,2,1,0,3:T(8,128)(2,1)} %get-tuple-element.6) | data formatting | bytes 4194304 | tf_op jit(solution)/shard_map/slice | solution.py:36
  111.8 2.3 %squeeze.17 = bf16[16,16,4096]{2,1,0:T(8,128)(2,1)} reshape(bf16[1,16,16,16,256]{4,3,2,1,0:T(8,128)(2,1)S(1)} %copy.9) | data formatting | bytes 4194304 | tf_op jit(solution)/shard_map/squeeze | solution.py:36
  114.2 4.2 %fusion.2 = f32[16,32,16]{1,2,0:T(8,128)S(1)} fusion(bf16[16,16,4096]{2,1,0:T(8,128)(2,1)} %squeeze.19, bf16[2,16,32,4096]{3,2,1,0:T(8,128)(2,1)} %param.4), kind=kOutput, calls=%fused_computation.2 | convolution fusion | flops 67108864 | bytes 6324224 | tf_op jit(solution)/shard_map/krs,kqs->krq/dot_general | solution.py:38
  118.4 3.6 %fusion = f32[16,32,16]{1,2,0:T(8,128)S(1)} fusion(bf16[16,16,4096]{2,1,0:T(8,128)(2,1)S(1)} %copy-done.1, bf16[2,16,32,4096]{3,2,1,0:T(8,128)(2,1)} %param.4), kind=kOutput, calls=%fused_computation | convolution fusion | flops 67108864 | bytes 6324224 | tf_op jit(solution)/shard_map/krs,kqs->krq/dot_general | solution.py:44
  121.9 3.6 %fusion.20 = f32[1,16,32,16]{2,3,1,0:T(8,128)S(1)} fusion(f32[16,32,16]{1,2,0:T(8,128)S(1)} %fusion.2, bf16[16,16,4096]{2,1,0:T(8,128)(2,1)S(1)} %copy-done.1, bf16[2,16,32,4096]{3,2,1,0:T(8,128)(2,1)} %param.4), kind=kOutput, calls=%fused_computation.22 | convolution fusion | flops 67117056 | bytes 6356992 | tf_op jit(solution)/shard_map/krs,kqs->krq/dot_general | solution.py:35
  125.5 1.2 fusion.26
  126.8 0.5 copy.11
  127.2 0.9 reshape.21
  128.1 9.6 %all-to-all-start.1 = ((f32[16,1,1024]{2,1,0:T(1,128)}), f32[16,1,1024]{2,1,0:T(1,128)S(1)}, u32[]{:S(2)}, u32[]{:S(2)}) async-start(f32[16,1,1024]{2,1,0:T(1,128)} %reshape.21), calls=%async_computation.1 | async-start | bytes 131072 | tf_op jit(solution)/shard_map/all_to_all | solution.py:49
  137.7 4.1 %negate_multiply_fusion = (f32[256,1024]{1,0:T(8,128)S(1)}, f32[256,1024]{1,0:T(8,128)S(1)}) fusion(), kind=kLoop, calls=%fused_computation.28 | loop fusion | flops 4456448 | bytes 2097152 | tf_op jit(solution)/shard_map/mul | solution.py:16
  141.9 3.2 %all-to-all-done.1 = f32[16,1,1024]{2,1,0:T(1,128)S(1)} async-done(((f32[16,1,1024]{2,1,0:T(1,128)}), f32[16,1,1024]{2,1,0:T(1,128)S(1)}, u32[]{:S(2)}, u32[]{:S(2)}) %all-to-all-start.1) | async-done | bytes 65568 | tf_op jit(solution)/shard_map/all_to_all | solution.py:49
  145.0 0.5 broadcast.22
  145.5 0.8 reduce
  146.3 0.2 reshape.22
  146.5 0.4 copy.13
  147.0 0.3 reshape.19
  147.3 1.3 fusion.16
  148.6 0.8 copy.14
  (14 shorter events, 0.1 us)
Async XLA Ops:
  114.1 4.2 %copy-start.1 = (bf16[16,16,4096]{2,1,0:T(8,128)(2,1)S(1)}, bf16[16,16,4096]{2,1,0:T(8,128)(2,1)}, u32[]{:S(2)}) copy-start(bf16[16,16,4096]{2,1,0:T(8,128)(2,1)} %squeeze.17) | copy-start | bytes 6291460
  114.2 11.3 %slice-start = ((s8[8388608]{0:T(1024)(128)(4,1)}), s8[4194304]{0:T(1024)(128)(4,1)S(1)}, s32[]{:S(2)}) async-start(s8[8388608]{0:T(1024)(128)(4,1)} %bitcast.59), calls=%async_computation.2 | async-start | bytes 8388608
  118.4 7.1 %slice-start.1 = ((s8[8388608]{0:T(1024)(128)(4,1)}), s8[4194304]{0:T(1024)(128)(4,1)S(1)}, s32[]{:S(2)}) async-start(s8[8388608]{0:T(1024)(128)(4,1)} %bitcast.59), calls=%async_computation.3 | async-start | bytes 8388608
  121.9 3.6 %copy-start = (bf16[16,16,4096]{2,1,0:T(8,128)(2,1)S(1)}, bf16[16,16,4096]{2,1,0:T(8,128)(2,1)}, u32[]{:S(2)}) copy-start(bf16[16,16,4096]{2,1,0:T(8,128)(2,1)} %squeeze.19) | copy-start | bytes 6291460
  128.1 16.9 %all-to-all-start.1 = ((f32[16,1,1024]{2,1,0:T(1,128)}), f32[16,1,1024]{2,1,0:T(1,128)S(1)}, u32[]{:S(2)}, u32[]{:S(2)}) async-start(f32[16,1,1024]{2,1,0:T(1,128)} %reshape.21), calls=%async_computation.1 | async-start | bytes 131072 | tf_op jit(solution)/shard_map/all_to_all | solution.py:49
  137.7 9.6 %copy-start.2 = (s32[16,2]{0,1:T(2,128)S(1)}, s32[16,2]{0,1:T(2,128)}, u32[]{:S(2)}) copy-start(s32[16,2]{0,1:T(2,128)} %param.7) | copy-start | bytes 388
  137.7 9.6 %copy-start.3 = (s32[16,2]{0,1:T(2,128)S(1)}, s32[16,2]{0,1:T(2,128)}, u32[]{:S(2)}) copy-start(s32[16,2]{0,1:T(2,128)} %param.6) | copy-start | bytes 388
